TPU v7x, 512 devices: a whole 4x4x16 slice. The times are simulated.
512 devices in a mesh: grp: 16 (over x, y), row: 8 (over z_hi, core), col: 4 (over z_lo).
Axes of the slice: x: 4, y: 4, z: 16 (z_hi: 4, z_lo: 4; z = z_hi * 4 + z_lo), core: 2. Of those that a mesh axis runs over, the one named last changes fastest.
Arguments:
- coherency: bfloat16 [32, 8, 16, 512, 512], P('grp', None, None, 'row', 'col'), may hold values from -0.125 to 0.125
- station_gains: float32 [32, 8, 16, 512], P('grp', None, None, ('row', 'col')), may hold values from -6 to 6
- tangent: float32 [32, 8, 16, 512], P('grp', None, None, ('row', 'col')), may hold values from -6 to 6
- flag_mask: int32 [512, 512], P('row', 'col'), may hold values 0 or 1
- station_order: int32 [512], replicated, may hold values from 0 to 511, each once
Outputs:
- hessian_product: float32 [32, 8, 16, 512], P('grp', None, None, ('row', 'col'))
Inputs may be any that keep to these rules, and one draw needn't show every extreme that they name: `station_order`: each station stands at exactly one position.
All inputs are finite; a program needn't handle non-finite values. No bound on the sum of `flag_mask` on one device may be relied on, other than what follows from the above.
Results may differ from a plain program's by a relative error of at most 0.0003.
Values sent between devices are 32-bit elements; how exact they have to be, the bound alone decides.
A program may use at most 64 MiB of HBM per device.

v0:
```python
import jax
import jax.numpy as jnp
from jax import lax
from jax.sharding import PartitionSpec as P

POLY = 4


consensus_weight = 1.0


def list_product(left_side, right_side):
    result = [None] * 8
    for row_a in range(2):
        for col_b in range(2):
            real_sum = 0.0
            imag_sum = 0.0
            for middle in range(2):
                left_real = left_side[2 * row_a + middle]
                left_imag = left_side[4 + 2 * row_a + middle]
                right_real = right_side[2 * middle + col_b]
                right_imag = right_side[4 + 2 * middle + col_b]
                real_sum = real_sum + left_real * right_real - left_imag * right_imag
                imag_sum = imag_sum + left_real * right_imag + left_imag * right_real
            result[2 * row_a + col_b] = real_sum
            result[4 + 2 * row_a + col_b] = imag_sum
    return result


def list_hermitian(matrix):
    result = [None] * 8
    for row_a in range(2):
        for col_b in range(2):
            result[2 * row_a + col_b] = matrix[2 * col_b + row_a]
            result[4 + 2 * row_a + col_b] = -matrix[4 + 2 * col_b + row_a]
    return result


def make_basis(count):
    frequency = -1.0 + (2.0 * jnp.arange(count).astype(jnp.float32) + 1.0) / count
    columns = [jnp.ones_like(frequency)]
    for degree in range(1, POLY):
        columns.append(columns[-1] * frequency)
    return jnp.stack(columns, axis=1)


def solve_coefficients(freq_basis, moments):
    gram_matrix = jnp.dot(freq_basis.T, freq_basis, precision=lax.Precision.HIGHEST)
    factor = jnp.linalg.cholesky(gram_matrix)
    flattened = moments.reshape(moments.shape[0], -1)
    solved = jax.scipy.linalg.cho_solve((factor, True), flattened)
    return solved.reshape(moments.shape)


def direction_lists(channel_coh, left_gain, right_gain, left_tan, right_tan, index):
    coh_dir = lax.dynamic_index_in_dim(channel_coh, index, 1, keepdims=False).astype(jnp.float32)
    gain_row = lax.dynamic_index_in_dim(left_gain, index, 1, keepdims=False)
    gain_col = lax.dynamic_index_in_dim(right_gain, index, 1, keepdims=False)
    tan_row = lax.dynamic_index_in_dim(left_tan, index, 1, keepdims=False)
    tan_col = lax.dynamic_index_in_dim(right_tan, index, 1, keepdims=False)
    coherent = [coh_dir[comp] for comp in range(8)]
    gi_list = [gain_row[comp][:, None] for comp in range(8)]
    gj_list = [gain_col[comp][None, :] for comp in range(8)]
    vi_list = [tan_row[comp][:, None] for comp in range(8)]
    vj_list = [tan_col[comp][None, :] for comp in range(8)]
    model_left = list_product(gi_list, coherent)
    model_right = list_product(coherent, list_hermitian(gj_list))
    return (model_left, model_right, vi_list, vj_list)


def on_device(coherency, station_gains, tangent, flag_mask, station_order):
    channel_count, _, direction_count, tile_rows, tile_cols = coherency.shape
    owned_count = tangent.shape[3]
    gain_all, tangent_all = (
        lax.all_gather(station_gains, ("row", "col"), axis=3, tiled=True),
        lax.all_gather(tangent, ("row", "col"), axis=3, tiled=True),
    )
    stations = gain_all.shape[3]
    row_ids = lax.dynamic_slice_in_dim(station_order, lax.axis_index("row") * tile_rows, tile_rows)
    col_ids = lax.dynamic_slice_in_dim(station_order, lax.axis_index("col") * tile_cols, tile_cols)
    weight = flag_mask.astype(jnp.float32)
    term_list = []
    for channel in range(channel_count):
        channel_coh = coherency[channel]
        left_gain = jnp.take(gain_all[channel], row_ids, axis=2)
        right_gain = jnp.take(gain_all[channel], col_ids, axis=2)
        left_tan = jnp.take(tangent_all[channel], row_ids, axis=2)
        right_tan = jnp.take(tangent_all[channel], col_ids, axis=2)

        def forward(index, accumulated):
            model_left, model_right, vi_list, vj_list = direction_lists(
                channel_coh, left_gain, right_gain, left_tan, right_tan, index
            )
            first = list_product(vi_list, model_right)
            second = list_product(model_left, list_hermitian(vj_list))
            return tuple((accumulated[comp] + first[comp] + second[comp] for comp in range(8)))

        start = tuple((jnp.zeros((tile_rows, tile_cols), jnp.float32) for comp in range(8)))
        change = lax.fori_loop(0, direction_count, forward, start)
        weighted = [change[comp] * weight for comp in range(8)]
        weighted_herm = list_hermitian(weighted)

        def backward(index):
            model_left, model_right, vi_list, vj_list = direction_lists(
                channel_coh, left_gain, right_gain, left_tan, right_tan, index
            )
            row_terms = list_product(weighted, list_hermitian(model_right))
            col_terms = list_product(weighted_herm, model_left)
            row_part = jnp.stack([jnp.sum(row_terms[comp], axis=1) for comp in range(8)])
            col_part = jnp.stack([jnp.sum(col_terms[comp], axis=0) for comp in range(8)])
            return (row_part, col_part)

        row_parts, col_parts = lax.map(backward, jnp.arange(direction_count))
        placed = jnp.zeros((8, direction_count, stations), jnp.float32)
        placed = placed.at[:, :, row_ids].add(jnp.moveaxis(row_parts, 0, 1))
        placed = placed.at[:, :, col_ids].add(jnp.moveaxis(col_parts, 0, 1))
        term_list.append(placed)
    partial_value = jnp.stack(term_list)
    summed = lax.psum(partial_value, ("row", "col"))
    data_term = lax.dynamic_slice_in_dim(
        summed, lax.axis_index(("row", "col")) * owned_count, owned_count, 3
    )
    total_channels = channel_count * lax.axis_size("grp")
    freq_basis = make_basis(total_channels)
    local_basis = lax.dynamic_slice_in_dim(
        freq_basis, lax.axis_index("grp") * channel_count, channel_count, 0
    )
    local_moments = jnp.einsum(
        "fk,fcds->kcds", local_basis, tangent, precision=lax.Precision.HIGHEST
    )
    moments = lax.psum(local_moments, "grp")
    coefficients = solve_coefficients(freq_basis, moments)
    smooth = jnp.einsum("fk,kcds->fcds", local_basis, coefficients, precision=lax.Precision.HIGHEST)
    return data_term + consensus_weight * (tangent - smooth)


def solution(mesh):
    in_specs = (
        P("grp", None, None, "row", "col"),
        P("grp", None, None, ("row", "col")),
        P("grp", None, None, ("row", "col")),
        P("row", "col"),
        P(),
    )
    out_specs = P("grp", None, None, ("row", "col"))
    return jax.shard_map(
        on_device, mesh=mesh, in_specs=in_specs, out_specs=out_specs, check_vma=False
    )
```

profile of v0, /device:TPU:1, one launch (start us, length us, event | category | flops | bytes accessed | tf_op | source)
XLA Modules:
  0.0 937.4 jit_solution(1265096757294552572)
XLA Ops:
  8.9 104.6 %all_gather.6 = f32[2,8,16,512]{2,1,3,0:T(8,128)S(1)} all-gather(f32[2,8,16,16]{2,1,3,0:T(8,128)S(1)} %copy.100), channel_id=1, replica_groups=mesh['grp'=16,'row'=8,'col'=4] {'row','col'}, dimensions={3}, use_global_device_ids=true | all-gather | bytes 540672 | tf_op jit(solution)/shard_map/all_gather | solution.py:75
  113.5 1.6 slice_bitcast_fusion.35
  115.2 97.2 %all_gather.7 = f32[2,8,16,512]{2,1,3,0:T(8,128)S(1)} all-gather(f32[2,8,16,16]{2,1,3,0:T(8,128)S(1)} %copy.101), channel_id=1, replica_groups=mesh['grp'=16,'row'=8,'col'=4] {'row','col'}, dimensions={3}, use_global_device_ids=true | all-gather | bytes 540672 | tf_op jit(solution)/shard_map/all_gather | solution.py:76
  212.4 2.3 slice_bitcast_fusion.34
  214.7 2.2 gather_fusion.6
  216.9 2.2 gather_fusion.1
  219.9 3.0 gather_fusion.3
  222.9 3.0 gather_fusion.4
  225.9 2.2 gather_fusion.5
  228.1 3.1 gather_fusion.7
  231.8 1.6 gather_fusion
  235.2 1.6 select_bitcast_fusion.2
  239.2 5.0 slice_bitcast_fusion.37
  244.2 158.0 %while.83 = (s32[]{:T(128)}, f32[64,128]{1,0:T(8,128)S(1)}, f32[64,128]{1,0:T(8,128)S(1)}, f32[64,128]{1,0:T(8,128)}, f32[64,128]{1,0:T(8,128)}, /*index=5*/f32[...) while((s32[]{:T(128)}, f32[64,128]{1,0:T(8,128)S(1)}, ...), condition=%wide.region_23.26_spmd.clone, body=%wide.region_22.25_spmd.clone.sunk | while | flops 2098186 | bytes 3870461 | solution.py:99
  256.8 1.6 fusion.203
  259.8 1.5 fusion.205
  266.7 1.6 fusion.203
  269.7 1.5 fusion.205
  276.6 1.6 fusion.203
  279.6 1.5 fusion.205
  286.5 1.6 fusion.203
  296.4 1.6 fusion.203
  299.4 1.5 fusion.205
  306.3 1.6 fusion.203
  309.3 1.5 fusion.205
  316.2 1.6 fusion.203
  319.2 1.5 fusion.205
  326.1 1.6 fusion.203
  329.1 1.5 fusion.205
  336.0 1.6 fusion.203
  339.0 1.5 fusion.205
  345.9 1.6 fusion.203
  348.9 1.5 fusion.205
  355.8 1.6 fusion.203
  365.6 1.6 fusion.203
  375.5 1.6 fusion.203
  385.4 1.6 fusion.203
  395.3 1.6 fusion.203
  402.2 1.9 copy.104
  406.2 102.9 %while.82 = (s32[]{:T(128)}, f32[64,128]{1,0:T(8,128)S(1)}, f32[64,128]{1,0:T(8,128)S(1)}, f32[64,128]{1,0:T(8,128)S(1)}, f32[64,128]{1,0:T(8,128)S(1)}, /*index...) while((s32[]{:T(128)}, f32[64,128]{1,0:T(8,128)S(1)}, ...), condition=%wide.region_1.4_spmd.clone, body=%wide.region_0.3_spmd.clone.sunk | while | flops 2098186 | bytes 3853741 | solution.py:99
  413.8 1.5 fusion.194
  420.3 1.5 fusion.194
  426.8 1.5 fusion.194
  433.4 1.5 fusion.194
  439.9 1.5 fusion.194
  446.4 1.5 fusion.194
  452.9 1.5 fusion.194
  459.4 1.5 fusion.194
  466.0 1.5 fusion.194
  472.5 1.5 fusion.194
  479.0 1.5 fusion.194
  485.5 1.5 fusion.194
  492.0 1.5 fusion.194
  498.5 1.5 fusion.194
  505.1 1.5 fusion.194
  510.1 91.8 %while.80 = (s32[]{:T(128)}, f32[16,8,64]{2,1,0:T(8,128)S(1)}, f32[16,8,128]{2,1,0:T(8,128)S(1)}, s32[16]{0:T(128)S(1)}, bf16[8,16,64,128]{3,2,1,0:T(8,128)(2,1)...) while((s32[]{:T(128)}, f32[16,8,64]{2,1,0:T(8,128)S(1)}, ...), condition=%wide.region_19.22_spmd, body=%wide.region_2.21_spmd.sunk | while | flops 2063372 | bytes 3467723 | solution.py:113
  602.6 2.7 scatter_fusion
  605.3 4.9 scatter_fusion.1
  610.9 94.5 %while.81 = (s32[]{:T(128)}, f32[16,8,64]{2,1,0:T(8,128)S(1)}, f32[16,8,128]{2,1,0:T(8,128)S(1)}, s32[16]{0:T(128)S(1)}, bf16[8,16,64,128]{3,2,1,0:T(8,128)(2,1)...) while((s32[]{:T(128)}, f32[16,8,64]{2,1,0:T(8,128)S(1)}, ...), condition=%wide.region_41.44_spmd, body=%wide.region_24.43_spmd.sunk | while | flops 2063372 | bytes 3467723 | solution.py:113
  706.7 2.7 scatter_fusion.2
  709.4 9.5 %scatter_fusion.3 = f32[8,16,512]{1,0,2:T(8,128)S(1)} fusion(f32[8,16,512]{1,0,2:T(8,128)S(1)} %scatter_fusion.2, s32[128]{0:T(128)S(1)} %copy-done.28, f32[128,8,16]{2,1,0:T(8,128)} %copy.118), kind=kCustom, calls=%fused_computation.11 | custom fusion | flops 16384 | bytes 197120 | tf_op jit(solution)/shard_map/scatter-add | solution.py:116
  724.0 62.4 %psum.15 = f32[8,16,16,4]{2,3,1,0:T(4,128)S(1)} all-reduce(f32[8,16,16,4]{2,3,1,0:T(4,128)S(1)} %copy.125), channel_id=1, replica_groups=mesh['grp'=16,'row'=8,'col'=4] {'grp'}, use_global_device_ids=true, to_apply=%region_47.50 | all-reduce | flops 8192 | bytes 65536 | tf_op jit(solution)/shard_map/psum | solution.py:131
  788.3 140.5 %all-reduce.2.cloned.1.call-done = f32[2,8,16,512]{3,2,1,0:T(8,128)} async-done(((f32[2,8,16,512]{3,2,1,0:T(8,128)}), f32[2,8,16,512]{3,2,1,0:T(8,128)}) %all-reduce.2.cloned.1.call-update) | async-done | bytes 524304 | tf_op jit(solution)/shard_map/psum | solution.py:119
  928.9 1.7 fusion.136
  (1400 shorter events, 342.5 us)
Async XLA Ops:
  6.5 922.3 %all-reduce.2.cloned.1.call-start = ((), (), s32[]{:S(2)}) async-start(), calls=%async_computation | async-start | bytes 1048576 | tf_op jit(solution)/shard_map/psum | solution.py:119
  256.7 6.5 copy-start.16
  256.7 6.5 copy-start.17
  256.8 6.5 copy-start.18
  256.8 6.5 copy-start.19
  266.6 6.5 copy-start.16
  266.6 6.5 copy-start.17
  266.7 6.5 copy-start.18
  266.7 6.5 copy-start.19
  276.5 6.5 copy-start.16
  276.5 6.5 copy-start.17
  276.5 6.5 copy-start.18
  276.6 6.5 copy-start.19
  286.4 6.5 copy-start.16
  286.4 6.5 copy-start.17
  286.4 6.5 copy-start.18
  286.5 6.5 copy-start.19
  296.3 6.5 copy-start.16
  296.3 6.5 copy-start.17
  296.3 6.5 copy-start.18
  296.4 6.5 copy-start.19
  306.2 6.5 copy-start.16
  306.2 6.5 copy-start.17
  306.2 6.5 copy-start.18
  306.2 6.5 copy-start.19
  316.1 6.5 copy-start.16
  316.1 6.5 copy-start.17
  316.1 6.5 copy-start.18
  316.1 6.5 copy-start.19
  326.0 6.5 copy-start.16
  326.0 6.5 copy-start.17
  326.0 6.5 copy-start.18
  326.0 6.5 copy-start.19
  335.9 6.5 copy-start.16
  335.9 6.5 copy-start.17
  335.9 6.5 copy-start.18
  335.9 6.5 copy-start.19
  345.8 6.5 copy-start.16
  345.8 6.5 copy-start.17
  345.8 6.5 copy-start.18
  345.8 6.5 copy-start.19
  355.7 6.5 copy-start.16
  355.7 6.5 copy-start.17
  355.7 6.5 copy-start.18
  355.7 6.5 copy-start.19
  365.6 6.5 copy-start.16
  365.6 6.5 copy-start.17
  365.6 6.5 copy-start.18
  365.6 6.5 copy-start.19
  375.5 6.5 copy-start.16
  375.5 6.5 copy-start.17
  375.5 6.5 copy-start.18
  375.5 6.5 copy-start.19
  385.3 6.5 copy-start.16
  385.4 6.5 copy-start.17
  385.4 6.5 copy-start.18
  385.4 6.5 copy-start.19
  395.2 6.5 copy-start.16
  406.1 102.9 %copy-start.2 = (f32[64,128]{1,0:T(8,128)S(1)}, f32[64,128]{1,0:T(8,128)}, u32[]{:S(2)}) copy-start(f32[64,128]{1,0:T(8,128)} %get-tuple-element.689) | copy-start | bytes 98308
  406.1 102.9 %copy-start.3 = (f32[64,128]{1,0:T(8,128)S(1)}, f32[64,128]{1,0:T(8,128)}, u32[]{:S(2)}) copy-start(f32[64,128]{1,0:T(8,128)} %get-tuple-element.691) | copy-start | bytes 98308
  406.1 102.9 %copy-start.8 = (f32[64,128]{1,0:T(8,128)S(1)}, f32[64,128]{1,0:T(8,128)}, u32[]{:S(2)}) copy-start(f32[64,128]{1,0:T(8,128)} %get-tuple-element.688) | copy-start | bytes 98308
  406.1 102.9 %copy-start.9 = (f32[64,128]{1,0:T(8,128)S(1)}, f32[64,128]{1,0:T(8,128)}, u32[]{:S(2)}) copy-start(f32[64,128]{1,0:T(8,128)} %get-tuple-element.690) | copy-start | bytes 98308
  406.2 102.9 %copy-start.10 = (f32[64,128]{1,0:T(8,128)S(1)}, f32[64,128]{1,0:T(8,128)}, u32[]{:S(2)}) copy-start(f32[64,128]{1,0:T(8,128)} %get-tuple-element.692) | copy-start | bytes 98308
  406.2 102.9 %copy-start.24 = (s32[64,128]{1,0:T(8,128)S(1)}, s32[64,128]{1,0:T(8,128)}, u32[]{:S(2)}) copy-start(s32[64,128]{1,0:T(8,128)} %param.20) | copy-start | bytes 98308
  (206 other events, 1059.7 us)
Sparse Core Ops, SparseCore 0:
  720.6 208.1 all-reduce.1
where the time goes:
time: 951 us; the launch traced here: 937 us
  other arithmetic  319 us (34%)
  blocking collectives  264 us (28%)
  waiting for transfers between devices  141 us (15%)
  local copies, waits for them, and re-layouts  131 us (14%)
  loops' own time  65.7 us (7%)
  between operations  13.9 us (1%)
    add x224, other arithmetic, forward(): accumulated[comp] + first[comp] + second[comp]  158 us
    psum x1, waiting for transfers between devices, on_device(): summed = lax.psum(partial_value, ('row', 'col'))  141 us
    all_gather x1, blocking collectives, on_device(): lax.all_gather(station_gains, ('row', 'col'), axis=3, tiled=True)  105 us
    all_gather x1, blocking collectives, on_device(): lax.all_gather(tangent, ('row', 'col'), axis=3, tiled=True)  97.2 us
    psum x1, blocking collectives, on_device(): moments = lax.psum(local_moments, 'grp')  62.4 us
    mul x64, other arithmetic, list_product(): real_sum = real_sum + left_real * right_real - left_imag * right_imag  61.1 us
    another operation x2, loops' own time, on_device(): row_parts, col_parts = lax.map(backward, jnp.arange(direction_count))  60.9 us
    mul x64, local copies, waits for them, and re-layouts, list_product(): real_sum = real_sum + left_real * right_real - left_imag * right_imag  59.1 us
  transfers between devices with their start and end apart: 1, of which 1 were waited for; matrix products, arithmetic and copies ran while one was open for 1% of the time, Pallas kernels for 0%

commit v1 on v0

v1 whole, which is shorter than its diff:
```python
import functools

import jax
import jax.numpy as jnp
import numpy as np
from jax import lax
from jax.experimental import pallas as pl
from jax.experimental.pallas import tpu as pltpu
from jax.sharding import PartitionSpec as P

POLY = 4
CONSENSUS_WEIGHT = 1.0
MESH = pl.DeviceIdType.MESH

COMPS = 8
CHIPS = 16
HALF = CHIPS // 2
NEAR = 4


def smooth_basis(count):
    frequency = -1.0 + (2.0 * np.arange(count) + 1.0) / count
    factor = np.linalg.cholesky(np.linalg.inv(np.vander(frequency, POLY, True).T @ np.vander(frequency, POLY, True))[::-1, ::-1])
    return [[float(value) for value in row] for row in factor.T[::-1, ::-1]]


class Place:
    def __init__(self):
        row, col = lax.axis_index("row"), lax.axis_index("col")
        self.core = lax.rem(row, 2)
        self.chip = (row // 2) * NEAR + col

    def at(self, step):
        return lax.rem(self.chip + (step + CHIPS), CHIPS)

    def neighbour(self, step):
        chip = self.at(step)
        return {"row": (chip // NEAR) * 2 + self.core, "col": lax.rem(chip, NEAR)}

    def sibling(self):
        chip = self.chip
        return {"row": (chip // NEAR) * 2 + (1 - self.core), "col": lax.rem(chip, NEAR)}


def entry(matrix, row, col, turned):
    if turned:
        return matrix[2 * col + row], matrix[4 + 2 * col + row], -1
    return matrix[2 * row + col], matrix[4 + 2 * row + col], 1


def add(total, term, sign):
    if total is None:
        return term if sign > 0 else -term
    return total + term if sign > 0 else total - term


def product(left_side, right_side, start=None, left_turned=False, right_turned=False):
    result = [None] * 8
    for row in range(2):
        for col in range(2):
            real, imag = (None, None) if start is None else (start[2 * row + col], start[4 + 2 * row + col])
            for middle in range(2):
                lr, li, ls = entry(left_side, row, middle, left_turned)
                rr, ri, rs = entry(right_side, middle, col, right_turned)
                real = add(add(real, lr * rr, 1), li * ri, -ls * rs)
                terms = [(lr * ri, rs), (li * rr, ls)]
                for term, sign in sorted(terms, key=lambda pair: -pair[1]):
                    imag = add(imag, term, sign)
            result[2 * row + col] = real
            result[4 + 2 * row + col] = imag
    return result


def split(value):
    high = value.astype(jnp.bfloat16)
    return high, (value - high.astype(jnp.float32)).astype(jnp.bfloat16)


def dot(left_side, right_side):
    return jnp.dot(left_side, right_side, preferred_element_type=jnp.float32)


ROWS = 16


REACH = 3
FAR = 4


def kernel(groups, gain_in, tan_in, order_in, flag_in, coh_in, out_ref,
           gain_ref, tan_ref, order_ref, flag_ref, coh_ref, all_ref, peer_buf, resid_ref,
           pick_ref, place_ref, mix_ref, gj_ref, left_ref, right_ref, row_ref, col_ref,
           part_ref, from_sib, total, far_buf, near_buf,
           in_sem, coh_sem, send_z, recv_z, send_s, recv_s, send_g, recv_g, send_w, recv_w, send_f, recv_f, send_n, recv_n):
    channels, comps, directions, tile_rows, tile_cols = coh_ref.shape
    stations = pick_ref.shape[1]
    values = comps * directions
    owned = gain_ref.shape[2]
    strips = tile_rows // ROWS
    place = Place()
    grp, row, col = lax.axis_index("grp"), lax.axis_index("row"), lax.axis_index("col")
    sibling = place.sibling()

    inputs = [
        pltpu.make_async_copy(source, target, in_sem.at[n])
        for n, (source, target) in enumerate(((gain_in, gain_ref), (tan_in, tan_ref), (order_in, order_ref), (flag_in, flag_ref)))
    ]
    for copy in inputs:
        copy.start()

    def peer(step):
        return {"grp": lax.rem(grp + (step + groups), groups)}

    partners = [place.neighbour(way * step) for step in range(1, max(REACH, FAR) + 1) for way in (1, -1)]
    partners = partners + [sibling] + [peer(step) for step in range(1, groups)]
    barrier = pltpu.get_barrier_semaphore()
    for device in partners:
        pl.semaphore_signal(barrier, inc=1, device_id=device, device_id_type=MESH)


    def block(channel, chip, core):
        start = pl.multiple_of(lax.rem(chip, NEAR) * owned, owned)
        return all_ref.at[channel, chip // NEAR, core, pl.ds(start, owned), :]

    def block_copy(channel, origin, core, target, send_sem, recv_sem):
        chip = place.at(origin)
        return pltpu.make_async_remote_copy(
            src_ref=block(channel, chip, core), dst_ref=block(channel, chip, core),
            send_sem=send_sem, recv_sem=recv_sem, device_id=target, device_id_type=MESH,
        )

    def limit(way):
        return HALF if way > 0 else HALF - 1

    def pass_on(channel, way, done):
        copies = []
        for step in range(REACH, 0, -1):
            if done + step <= limit(way):
                slot = HALF + way * (done + step)
                copies.append(block_copy(
                    channel, -way * done, place.core, place.neighbour(way * step), send_z.at[channel, slot], recv_z.at[channel, slot]
                ))
        return copies

    def to_sibling(channel, offset):
        slot = HALF + offset
        return block_copy(channel, -offset, place.core, sibling, send_s.at[channel, slot], recv_s.at[channel, slot])

    def from_ring(channel, offset):
        slot = HALF + offset
        return block_copy(channel, -offset, place.core, sibling, send_z.at[channel, slot], recv_z.at[channel, slot])

    def from_sibling(channel, offset):
        slot = HALF + offset
        return block_copy(channel, -offset, 1 - place.core, sibling, send_s.at[channel, slot], recv_s.at[channel, slot])

    offsets = range(1 - HALF, HALF + 1)
    stages = -(-HALF // REACH)

    def begin_gather(channel):
        for copy in pass_on(channel, 1, 0) + pass_on(channel, -1, 0) + [to_sibling(channel, 0)]:
            copy.start()

    def gather_stage(channel, stage):
        for distance in range(min((stage + 1) * REACH, HALF), stage * REACH, -1):
            for way in (1, -1):
                if distance <= limit(way):
                    from_ring(channel, way * distance).wait_recv()
                    if distance % REACH == 0:
                        for copy in pass_on(channel, way, distance):
                            copy.start()
                    to_sibling(channel, way * distance).start()

    def end_gather(channel):
        for offset in offsets:
            from_sibling(channel, offset).wait_recv()

    def to_peer(step):
        return pltpu.make_async_remote_copy(
            src_ref=peer_buf.at[0], dst_ref=peer_buf.at[step],
            send_sem=send_g.at[step], recv_sem=recv_g.at[step], device_id=peer(step), device_id_type=MESH,
        )

    def gather_sends(channel):
        copies = [to_sibling(channel, offset) for offset in offsets]
        for way in (1, -1):
            for done in range(0, limit(way), REACH):
                copies += pass_on(channel, way, done)
        return copies


    def rows_of(step):
        chip = place.at(step)
        return chip // NEAR, pl.ds(pl.multiple_of(lax.rem(chip, NEAR) * owned, owned), owned)

    def sums_for(channel, step):
        run, rows = rows_of(step)
        return total.at[channel, run, rows, :]

    def swap(channel):
        return pltpu.make_async_remote_copy(
            src_ref=part_ref.at[channel, :, 1 - place.core], dst_ref=from_sib.at[channel],
            send_sem=send_w.at[channel], recv_sem=recv_w.at[channel], device_id=sibling, device_id_type=MESH,
        )

    def hop(channel, source, buffer, slot, sends, recvs, step):
        return pltpu.make_async_remote_copy(
            src_ref=source, dst_ref=buffer.at[channel, slot], send_sem=sends.at[channel, slot], recv_sem=recvs.at[channel, slot],
            device_id=place.neighbour(step), device_id_type=MESH,
        )

    reaches = ((1, HALF - FAR), (-1, HALF - 1 - FAR))

    def to_add(channel):
        return {
            way * step: hop(channel, sums_for(channel, way * (step + FAR)), far_buf, FAR + way * step, send_f, recv_f, way * step)
            for way, most in reaches for step in range(most, 0, -1)
        }

    def direct(channel):
        return {
            way * step: hop(channel, sums_for(channel, way * step), near_buf, FAR + way * step, send_n, recv_n, way * step)
            for step in range(1, FAR) for way in (1, -1)
        }

    def added(channel):
        return {
            way * FAR: hop(channel, far_buf.at[channel, FAR if way > 0 else 2 * FAR + 1], near_buf, FAR + way * FAR, send_n, recv_n, way * FAR)
            for way in (1, -1)
        }

    def send_sums(channel):
        swap(channel).wait_recv()
        total[channel] = part_ref[channel, :, place.core] + from_sib[channel]
        for copy in list(to_add(channel).values()) + list(direct(channel).values()):
            copy.start()

    def send_added(channel):
        arrivals = to_add(channel)
        for (way, most), copy in zip(reaches, added(channel).values()):
            run, rows = rows_of(way * FAR)
            gathered = total[channel, run, rows, :]
            for step in range(1, most + 1):
                arrivals[way * step].wait_recv()
                gathered = gathered + far_buf[channel, FAR + way * step]
            far_buf[channel, FAR if way > 0 else 2 * FAR + 1] = gathered
            copy.start()

    def finish(channel):
        run, rows = rows_of(0)
        summed = total[channel, run, rows, :] + resid_ref[channel]
        for copy in list(direct(channel).values()) + list(added(channel).values()):
            copy.wait_recv()
        for slot in range(2 * FAR + 1):
            if slot != FAR:
                summed = summed + near_buf[channel, slot]
        out_ref[channel] = summed.T

    def sum_sends(channel):
        return [swap(channel)] + list(to_add(channel).values()) + list(direct(channel).values()) + list(added(channel).values())


    basis = smooth_basis(channels * groups)

    def heights(group, channel):
        frequency = (group * channels + channel).astype(jnp.float32) * (2.0 / (channels * groups)) + (1.0 / (channels * groups) - 1.0)
        powers = [1.0]
        for _ in range(1, POLY):
            powers.append(powers[-1] * frequency)
        return [sum(line[k] * powers[k] for k in range(POLY) if abs(line[k]) > 1e-9) for line in basis]

    def consensus():
        moments = [jnp.zeros((owned, values), jnp.float32) for _ in range(POLY)]
        for step in range(groups):
            if step > 0:
                to_peer(step).wait_recv()
            origin = lax.rem(grp + (groups - step), groups)
            for source in range(channels):
                seen = peer_buf[step, source]
                for k, height in enumerate(heights(origin, source)):
                    moments[k] = moments[k] + height * seen
        for channel in range(channels):
            smooth = sum(height * moment for height, moment in zip(heights(grp, channel), moments))
            resid_ref[channel] = CONSENSUS_WEIGHT * (peer_buf[0, channel] - smooth)


    lane = lax.broadcasted_iota(jnp.int32, (ROWS, 128), 1)
    same_row = (lane & (ROWS - 1)) == lax.broadcasted_iota(jnp.int32, (ROWS, 128), 0)

    def as_mask(hit):
        return hit.astype(jnp.float32).astype(jnp.bfloat16)

    def one_hots():
        col_ids = order_ref[pl.ds(col, 1), :]
        row_ids = order_ref[pl.ds(row // 2, 1), :]
        row_ids = jnp.where(lax.rem(row, 2) == 1, pltpu.roll(row_ids, tile_rows, 1), row_ids)
        for n, ids in enumerate((col_ids, row_ids)):
            ids = jnp.broadcast_to(ids, (128, 128))
            turned = ids.astype(jnp.float32).T.astype(jnp.int32)
            count = (tile_cols, tile_rows)[n]
            for tile in range(stations // 128):
                spot = lax.broadcasted_iota(jnp.int32, (128, 128), 1) + tile * 128
                pick_ref[n * tile_cols:n * tile_cols + count, tile * 128:(tile + 1) * 128] = as_mask(turned == spot)[:count]
                spot = lax.broadcasted_iota(jnp.int32, (128, 128), 0) + tile * 128
                place_ref[tile * 128:(tile + 1) * 128, n * 128:(n + 1) * 128] = as_mask(ids == spot)

    def prologue(channel):
        parts = split(all_ref[channel].reshape(stations, 2 * values))
        chosen = [dot(pick_ref[...], part) for part in parts]

        chosen_cols = chosen[0][:tile_cols] + chosen[1][:tile_cols]
        for array in range(2):
            turned = chosen_cols[:, array * values:(array + 1) * values].T
            gj_ref[pl.ds(array * comps, comps)] = turned.reshape(comps, directions, tile_cols)

        sides = [[
            one[tile_cols:, array * values:(array + 1) * values].T.reshape(comps, directions, tile_rows) for array in range(2)
        ] for one in chosen]
        for index in range(strips):
            lanes = slice(index * ROWS, (index + 1) * ROWS)
            for array in range(2):
                for line in range(2):
                    for part in range(2):
                        pieces = []
                        for side in sides:
                            for middle in range(2):
                                for other in range(2):
                                    value = side[array][4 * (part ^ other) + 2 * line + middle][:, lanes]
                                    pieces.append(-value if (part, other) == (0, 1) else value)
                        mix_ref[index, 4 * array + 2 * line + part] = jnp.concatenate(pieces, axis=1)
        col_ref[...] = jnp.zeros_like(col_ref)

    def strip(channel, index):
        rows = pl.ds(pl.multiple_of(index * ROWS, ROWS), ROWS)

        def forward(direction, change):
            here = pl.ds(direction, 1)
            coherent = [coh_ref[channel, comp, direction, rows, :] for comp in range(comps)]
            stacked = jnp.concatenate([
                jnp.concatenate([coherent[4 * part + 2 * middle], coherent[4 * part + 2 * middle + 1]], axis=1)
                for middle in range(2) for part in range(2)
            ], axis=0)
            mixing = jnp.concatenate([
                jnp.where(same_row, mix_ref[index, n, here, :], 0.0).astype(jnp.bfloat16) for n in range(8)
            ], axis=0)
            models = dot(mixing, jnp.concatenate([stacked, stacked], axis=0))

            def model(array):
                return [
                    models[ROWS * (4 * array + 2 * line + part):ROWS * (4 * array + 2 * line + part + 1), end * 128:(end + 1) * 128]
                    for part in range(2) for line in range(2) for end in range(2)
                ]

            model_left, tan_left = model(0), model(1)
            gain_j = [gj_ref[comp, here, :] for comp in range(comps)]
            tan_j = [gj_ref[comps + comp, here, :] for comp in range(comps)]
            for comp in range(comps):
                left_ref[comp, direction] = model_left[comp]
            change = product(tan_left, gain_j, change, right_turned=True)
            change = product(model_left, tan_j, change, right_turned=True)
            model_right = product([value.astype(jnp.float32) for value in coherent], gain_j, right_turned=True)
            for part in range(2):
                for line in range(2):
                    for end in range(2):
                        for n, piece in enumerate(split(model_right[4 * part + 2 * line + end])):
                            right_ref[4 * n + 2 * line + part, direction, :, end * 128:(end + 1) * 128] = piece
            return tuple(change)

        zero = jnp.zeros((ROWS, tile_cols), jnp.float32)
        change = lax.fori_loop(0, directions, forward, (zero,) * comps, unroll=4)
        weight = flag_ref[rows, :].astype(jnp.float32)
        weighted = [value * weight for value in change]

        pieces = [split(value) for value in weighted]
        lines = jnp.concatenate([
            jnp.concatenate([pieces[4 * part + 2 * line][n], pieces[4 * part + 2 * line + 1][n]], axis=1)
            for n in range(2) for line in range(2) for part in range(2)
        ], axis=0)
        pairs = lax.dot_general(
            right_ref[...].reshape(2 * 4 * directions * ROWS, 2 * tile_cols), lines, (((1,), (1,)), ((), ())), preferred_element_type=jnp.float32
        ).reshape(2, 4, directions, ROWS, 128)
        for n in range(4):
            kept = jnp.where(same_row[None], pairs[0, n] + pairs[1, n], 0.0)
            row_ref[index, n] = jnp.sum(kept, axis=1)

        def backward(direction, _):
            model_left = [left_ref[comp, direction] for comp in range(comps)]
            terms = product(weighted, model_left, left_turned=True)
            for comp in range(comps):
                folded = terms[comp][:8]
                for part in range(1, ROWS // 8):
                    folded = folded + terms[comp][8 * part:8 * part + 8]
                col_ref[comp, direction] += folded
            return 0

        lax.fori_loop(0, directions, backward, 0, unroll=4)

    def epilogue(channel):
        sums = [[row_ref[index, n] for n in range(4)] for index in range(strips)]
        sums = [[value[:, :64] + value[:, 64:] for value in line] for line in sums]

        def cut(value, line, part):
            return value[:, (2 * line + part) * ROWS:(2 * line + part + 1) * ROWS]

        by_comp = []
        for part in range(2):
            for line in range(2):
                for end in range(2):
                    pieces = []
                    for value in sums:
                        if part == 0:
                            pieces.append(cut(value[2 * end], line, 0) + cut(value[2 * end + 1], line, 1))
                        else:
                            pieces.append(cut(value[2 * end], line, 1) - cut(value[2 * end + 1], line, 0))
                    by_comp.append(jnp.concatenate(pieces, axis=1))
        row_sums = jnp.concatenate(by_comp, axis=0)
        col_sums = jnp.sum(col_ref[...], axis=2).reshape(values, tile_cols)
        placed = jnp.zeros((stations, values), jnp.float32)
        for part in split(jnp.concatenate([col_sums, row_sums], axis=1)):
            placed = placed + lax.dot_general(
                place_ref[:, :tile_cols + tile_rows], part, (((1,), (1,)), ((), ())), preferred_element_type=jnp.float32
            )
        part_ref[channel] = placed.reshape(part_ref.shape[1:])
        swap(channel).start()


    inputs[0].wait()
    inputs[1].wait()
    own_start = pl.multiple_of(lax.rem(place.chip, NEAR) * owned, owned)
    for channel in range(channels):
        tan_t = tan_ref[channel].T
        peer_buf[0, channel] = tan_t
        own = all_ref.at[channel, place.chip // NEAR, place.core, pl.ds(own_start, owned), :]
        own[:, :values] = gain_ref[channel].T
        own[:, values:] = tan_t
    pl.semaphore_wait(barrier, len(partners))
    begin_gather(0)
    coherency = [pltpu.make_async_copy(coh_in.at[channel], coh_ref.at[channel], coh_sem.at[channel]) for channel in range(channels)]
    for copy in coherency:
        copy.start()
    inputs[2].wait()
    inputs[3].wait()
    one_hots()
    gather_stage(0, 0)
    begin_gather(1)
    for step in range(1, groups):
        to_peer(step).start()
    for stage in range(1, stages):
        gather_stage(0, stage)
    end_gather(0)
    for copy in coherency:
        copy.wait()

    def work(channel, _):
        @pl.when(channel == 1)
        def _():
            end_gather(1)

        prologue(channel)

        def one(index, _):
            for stage in range(stages):
                @pl.when(jnp.logical_and(channel == 0, index == stage))
                def _():
                    gather_stage(1, stage)

            @pl.when(jnp.logical_and(channel == 1, index == 0))
            def _():
                send_sums(0)

            @pl.when(jnp.logical_and(channel == 1, index == 1))
            def _():
                consensus()

            @pl.when(jnp.logical_and(channel == 1, index == 3))
            def _():
                send_added(0)

            strip(channel, index)
            return 0

        lax.fori_loop(0, strips, one, 0)
        epilogue(channel)
        return 0

    lax.fori_loop(0, channels, work, 0)
    send_sums(1)
    finish(0)
    send_added(1)
    finish(1)
    for channel in range(channels):
        for copy in gather_sends(channel) + sum_sends(channel):
            copy.wait_send()
    for step in range(1, groups):
        to_peer(step).wait_send()


def on_device(groups, coherency, station_gains, tangent, flag_mask, station_order):
    channels, comps, directions, tile_rows, tile_cols = coherency.shape
    owned = tangent.shape[3]
    stations = station_order.shape[0]
    values = comps * directions
    runs = CHIPS // NEAR
    near = NEAR * owned
    strips = tile_rows // ROWS
    vmem = pltpu.VMEM
    f32, bf16 = jnp.float32, jnp.bfloat16

    def sems(*shape):
        return pltpu.SemaphoreType.DMA(shape)

    hbm = pl.BlockSpec(memory_space=pl.ANY)
    result = pl.pallas_call(
        functools.partial(kernel, groups),
        out_shape=jax.ShapeDtypeStruct((channels, values, owned), f32),
        in_specs=[hbm] * 5,
        out_specs=pl.BlockSpec(memory_space=pltpu.VMEM),
        scratch_shapes=[
            vmem((channels, values, owned), f32),
            vmem((channels, values, owned), f32),
            vmem((stations // 128, 128), jnp.int32),
            vmem((tile_rows, tile_cols), jnp.int32),
            vmem(coherency.shape, bf16),
            vmem((channels, runs, 2, near, 2 * values), f32),
            vmem((groups, channels, owned, values), f32),
            vmem((channels, owned, values), f32),
            vmem((tile_cols + tile_rows, stations), bf16),
            vmem((stations, 256), bf16),
            vmem((strips, comps, directions, 128), f32),
            vmem((2 * comps, directions, tile_cols), f32),
            vmem((comps, directions, ROWS, tile_cols), f32),
            vmem((comps, directions, ROWS, 2 * tile_cols), bf16),
            vmem((strips, 4, directions, 128), f32),
            vmem((comps, directions, 8, tile_cols), f32),
            vmem((channels, runs, 2, near, values), f32),
            vmem((channels, runs, near, values), f32),
            vmem((channels, runs, near, values), f32),
            vmem((channels, 2 * FAR + 2, owned, values), f32),
            vmem((channels, 2 * FAR + 1, owned, values), f32),
            sems(4), sems(channels),
            sems(channels, CHIPS + 1), sems(channels, CHIPS + 1), sems(channels, CHIPS + 1), sems(channels, CHIPS + 1),
            sems(groups), sems(groups), sems(channels), sems(channels),
            sems(channels, 2 * FAR + 1), sems(channels, 2 * FAR + 1), sems(channels, 2 * FAR + 1), sems(channels, 2 * FAR + 1),
        ],
        compiler_params=pltpu.CompilerParams(collective_id=0, has_side_effects=True, vmem_limit_bytes=56 << 20),
        name="hessian",
    )(
        station_gains.reshape(channels, values, owned),
        tangent.reshape(channels, values, owned),
        station_order.reshape(stations // 128, 128),
        flag_mask,
        coherency,
    )
    return result.reshape(channels, comps, directions, owned)


def solution(mesh):
    in_specs = (
        P("grp", None, None, "row", "col"),
        P("grp", None, None, ("row", "col")),
        P("grp", None, None, ("row", "col")),
        P("row", "col"),
        P(),
    )
    out_specs = P("grp", None, None, ("row", "col"))
    return jax.shard_map(
        functools.partial(on_device, mesh.shape["grp"]),
        mesh=mesh, in_specs=in_specs, out_specs=out_specs, check_vma=False,
    )
```

time: 951 us -> 67.2 us (0.07); the launches traced: 937 us -> 67 us
  other arithmetic: 319 us -> 0 us
  blocking collectives: 264 us -> 0 us
  waiting for transfers between devices: 141 us -> 0 us
  local copies, waits for them, and re-layouts: 131 us -> 1.57 us
  loops' own time: 65.7 us -> 0 us
  Pallas kernels: 0 us -> 65.5 us
  between operations: 13.9 us -> 0.01 us
    all_gather x2 -> x0, blocking collectives: 202 us -> none  [the longest x1 105 us: on_device(): lax.all_gather(station_gains, ('row', 'col'), axis=3, tiled=True)]
    add x258 -> x0, other arithmetic: 163 us -> none  [the longest x224 158 us: forward(): accumulated[comp] + first[comp] + second[comp]]
    psum x1 -> x0, waiting for transfers between devices: 141 us -> none  [on_device(): summed = lax.psum(partial_value, ('row', 'col'))]
    another operation x4 -> x0, loops' own time: 65.7 us -> none  [the longest x2 60.9 us: on_device(): row_parts, col_parts = lax.map(backward, jnp.arange(direction_count))]
    pallas_call x0 -> x1, Pallas kernels: none -> 65.5 us  [on_device(): pl.pallas_call(functools.partial(kernel, groups), out_shape=jax.ShapeDtyp...]
    psum x1 -> x0, blocking collectives: 62.4 us -> none  [on_device(): moments = lax.psum(local_moments, 'grp')]
    mul x65 -> x0, other arithmetic: 61.1 us -> none  [the longest x64 61.1 us: list_product(): real_sum = real_sum + left_real * right_real - left_imag * right_imag]
    mul x64 -> x0, local copies, waits for them, and re-layouts: 59.1 us -> none  [list_product(): real_sum = real_sum + left_real * right_real - left_imag * right_imag]
  transfers between devices with their start and end apart: 1 -> 0, of which waited for: 1 -> 0; matrix products, arithmetic and copies ran while one was open for 1% -> 0% of each run, Pallas kernels for 0% -> 0%
where the time goes in v1:
time: 67.2 us; the launch traced here: 67 us
  Pallas kernels  65.5 us (97%)
  local copies, waits for them, and re-layouts  1.57 us (2%)
    pallas_call x1, Pallas kernels, on_device(): pl.pallas_call(functools.partial(kernel, groups), out_shape=jax.ShapeDtyp...  65.5 us
    unnamed x1, local copies, waits for them, and re-layouts  1.57 us

profile of v1, /device:TPU:1, one launch (start us, length us, event | category | flops | bytes accessed | tf_op | source)
XLA Modules:
  0.0 67.0 jit_solution(7955710806776327706)
XLA Ops:
  0.0 65.5 %hessian.1 = f32[2,128,16]{2,1,0:T(8,128)} custom-call(f32[2,128,16]{2,1,0:T(8,128)} %bitcast.5, f32[2,128,16]{2,1,0:T(8,128)} %bitcast.6, s32[4,128]{1,0:T(4,128)} %bitcast.7, s32[64,128]{1,0:T(8,128)} %flag_in.1, bf16[2,8,16,64,128]{4,3,2,1,0:T(8,128)(2,1)} %coh_in.1), custom_call_target="tpu_custom_call" | custom-call | tf_op jit(solution)/shard_map/hessian/pallas_call | solution.py:513
  65.5 1.6 %copy.7 = f32[2,8,16,16]{3,2,1,0:T(8,128)} copy(f32[2,8,16,16]{3,2,1,0:T(8,128)} %bitcast.4) | data formatting | bytes 32768

commit v2 on v1

--- a/solution.py
+++ b/solution.py
@@ -42,30 +42,32 @@
         return {"row": (chip // NEAR) * 2 + (1 - self.core), "col": lax.rem(chip, NEAR)}
 
 
-def entry(matrix, row, col, turned):
-    if turned:
-        return matrix[2 * col + row], matrix[4 + 2 * col + row], -1
-    return matrix[2 * row + col], matrix[4 + 2 * row + col], 1
-
-
-def add(total, term, sign):
-    if total is None:
-        return term if sign > 0 else -term
-    return total + term if sign > 0 else total - term
-
-
-def product(left_side, right_side, start=None, left_turned=False, right_turned=False):
+def factors(real, imag):
+    return real, imag - real, real + imag
+
+
+def conjugate_turned(matrix):
+    return [[factors(matrix[2 * col + row], -matrix[4 + 2 * col + row]) for col in range(2)] for row in range(2)]
+
+
+def summed_parts(matrix):
+    return [[(matrix[2 * row + col], matrix[4 + 2 * row + col], matrix[2 * row + col] + matrix[4 + 2 * row + col]) for col in range(2)] for row in range(2)]
+
+
+def products(pairs, start=None):
     result = [None] * 8
     for row in range(2):
         for col in range(2):
-            real, imag = (None, None) if start is None else (start[2 * row + col], start[4 + 2 * row + col])
-            for middle in range(2):
-                lr, li, ls = entry(left_side, row, middle, left_turned)
-                rr, ri, rs = entry(right_side, middle, col, right_turned)
-                real = add(add(real, lr * rr, 1), li * ri, -ls * rs)
-                terms = [(lr * ri, rs), (li * rr, ls)]
-                for term, sign in sorted(terms, key=lambda pair: -pair[1]):
-                    imag = add(imag, term, sign)
+            sums = [None] * 3
+            for left_side, right_side, turned in pairs:
+                for middle in range(2):
+                    left, right = left_side[row][middle], right_side[middle][col]
+                    (real, imag, both), (first, second, third) = (right, left) if turned else (left, right)
+                    for n, term in enumerate((first * both, second * real, third * imag)):
+                        sums[n] = term if sums[n] is None else sums[n] + term
+            real, imag = sums[0] - sums[2], sums[0] + sums[1]
+            if start is not None:
+                real, imag = start[2 * row + col] + real, start[4 + 2 * row + col] + imag
             result[2 * row + col] = real
             result[4 + 2 * row + col] = imag
     return result
@@ -83,7 +85,7 @@
 ROWS = 16
 
 
-REACH = 3
+REACH = 4
 FAR = 4
 
 
@@ -310,8 +312,11 @@
 
         chosen_cols = chosen[0][:tile_cols] + chosen[1][:tile_cols]
         for array in range(2):
-            turned = chosen_cols[:, array * values:(array + 1) * values].T
-            gj_ref[pl.ds(array * comps, comps)] = turned.reshape(comps, directions, tile_cols)
+            turned = chosen_cols[:, array * values:(array + 1) * values].T.reshape(comps, directions, tile_cols)
+            for line, entries in enumerate(conjugate_turned([turned[comp] for comp in range(comps)])):
+                for end, entry in enumerate(entries):
+                    for n, factor in enumerate(entry):
+                        gj_ref[12 * array + 6 * line + 3 * end + n] = factor
 
         sides = [[
             one[tile_cols:, array * values:(array + 1) * values].T.reshape(comps, directions, tile_rows) for array in range(2)
@@ -334,7 +339,7 @@
         rows = pl.ds(pl.multiple_of(index * ROWS, ROWS), ROWS)
 
         def forward(direction, change):
-            here = pl.ds(direction, 1)
+            here = slice(direction, direction + 1)
             coherent = [coh_ref[channel, comp, direction, rows, :] for comp in range(comps)]
             stacked = jnp.concatenate([
                 jnp.concatenate([coherent[4 * part + 2 * middle], coherent[4 * part + 2 * middle + 1]], axis=1)
@@ -352,48 +357,53 @@
                 ]
 
             model_left, tan_left = model(0), model(1)
-            gain_j = [gj_ref[comp, here, :] for comp in range(comps)]
-            tan_j = [gj_ref[comps + comp, here, :] for comp in range(comps)]
+            gain_j, tan_j = ([
+                [[gj_ref[12 * array + 6 * line + 3 * end + n, here, :] for n in range(3)] for end in range(2)] for line in range(2)
+            ] for array in range(2))
             for comp in range(comps):
                 left_ref[comp, direction] = model_left[comp]
-            change = product(tan_left, gain_j, change, right_turned=True)
-            change = product(model_left, tan_j, change, right_turned=True)
-            model_right = product([value.astype(jnp.float32) for value in coherent], gain_j, right_turned=True)
+            model_right = products([(summed_parts([value.astype(jnp.float32) for value in coherent]), gain_j, False)])
+            change = products([(summed_parts(tan_left), gain_j, False), (summed_parts(model_left), tan_j, False)], change)
             for part in range(2):
                 for line in range(2):
                     for end in range(2):
                         for n, piece in enumerate(split(model_right[4 * part + 2 * line + end])):
-                            right_ref[4 * n + 2 * line + part, direction, :, end * 128:(end + 1) * 128] = piece
+                            lanes = slice((2 * n + end) * tile_cols, (2 * n + end + 1) * tile_cols)
+                            right_ref[2 * line + part, direction, :, lanes] = piece
             return tuple(change)
 
         zero = jnp.zeros((ROWS, tile_cols), jnp.float32)
-        change = lax.fori_loop(0, directions, forward, (zero,) * comps, unroll=4)
+        change = (zero,) * comps
+        for direction in range(directions):
+            change = forward(direction, change)
         weight = flag_ref[rows, :].astype(jnp.float32)
         weighted = [value * weight for value in change]
 
         pieces = [split(value) for value in weighted]
+        lines = [
+            jnp.concatenate([
+                jnp.concatenate([pieces[4 * part + 2 * line][n], pieces[4 * part + 2 * line + 1][n]], axis=1)
+                for line in range(2) for part in range(2)
+            ], axis=0) for n in range(2)
+        ]
         lines = jnp.concatenate([
-            jnp.concatenate([pieces[4 * part + 2 * line][n], pieces[4 * part + 2 * line + 1][n]], axis=1)
-            for n in range(2) for line in range(2) for part in range(2)
+            jnp.concatenate([lines[0], lines[0]], axis=1), jnp.concatenate([lines[1], jnp.zeros_like(lines[1])], axis=1)
         ], axis=0)
         pairs = lax.dot_general(
-            right_ref[...].reshape(2 * 4 * directions * ROWS, 2 * tile_cols), lines, (((1,), (1,)), ((), ())), preferred_element_type=jnp.float32
-        ).reshape(2, 4, directions, ROWS, 128)
+            right_ref[...].reshape(4 * directions * ROWS, 4 * tile_cols), lines, (((1,), (1,)), ((), ())), preferred_element_type=jnp.float32
+        ).reshape(4, directions, ROWS, 128)
         for n in range(4):
-            kept = jnp.where(same_row[None], pairs[0, n] + pairs[1, n], 0.0)
-            row_ref[index, n] = jnp.sum(kept, axis=1)
-
-        def backward(direction, _):
+            row_ref[index, n] = jnp.sum(jnp.where(same_row[None], pairs[n], 0.0), axis=1)
+
+        turned = conjugate_turned(weighted)
+        for direction in range(directions):
             model_left = [left_ref[comp, direction] for comp in range(comps)]
-            terms = product(weighted, model_left, left_turned=True)
+            terms = products([(turned, summed_parts(model_left), True)])
             for comp in range(comps):
                 folded = terms[comp][:8]
                 for part in range(1, ROWS // 8):
                     folded = folded + terms[comp][8 * part:8 * part + 8]
                 col_ref[comp, direction] += folded
-            return 0
-
-        lax.fori_loop(0, directions, backward, 0, unroll=4)
 
     def epilogue(channel):
         sums = [[row_ref[index, n] for n in range(4)] for index in range(strips)]
@@ -468,10 +478,6 @@
             def _():
                 send_sums(0)
 
-            @pl.when(jnp.logical_and(channel == 1, index == 1))
-            def _():
-                consensus()
-
             @pl.when(jnp.logical_and(channel == 1, index == 3))
             def _():
                 send_added(0)
@@ -485,6 +491,7 @@
 
     lax.fori_loop(0, channels, work, 0)
     send_sums(1)
+    consensus()
     finish(0)
     send_added(1)
     finish(1)
@@ -509,7 +516,7 @@
     def sems(*shape):
         return pltpu.SemaphoreType.DMA(shape)
 
-    hbm = pl.BlockSpec(memory_space=pl.ANY)
+    hbm = pl.BlockSpec(memory_space=pltpu.HBM)
     result = pl.pallas_call(
         functools.partial(kernel, groups),
         out_shape=jax.ShapeDtypeStruct((channels, values, owned), f32),
@@ -527,9 +534,9 @@
             vmem((tile_cols + tile_rows, stations), bf16),
             vmem((stations, 256), bf16),
             vmem((strips, comps, directions, 128), f32),
-            vmem((2 * comps, directions, tile_cols), f32),
+            vmem((24, directions, tile_cols), f32),
             vmem((comps, directions, ROWS, tile_cols), f32),
-            vmem((comps, directions, ROWS, 2 * tile_cols), bf16),
+            vmem((4, directions, ROWS, 4 * tile_cols), bf16),
             vmem((strips, 4, directions, 128), f32),
             vmem((comps, directions, 8, tile_cols), f32),
             vmem((channels, runs, 2, near, values), f32),
@@ -542,14 +549,16 @@
             sems(groups), sems(groups), sems(channels), sems(channels),
             sems(channels, 2 * FAR + 1), sems(channels, 2 * FAR + 1), sems(channels, 2 * FAR + 1), sems(channels, 2 * FAR + 1),
         ],
-        compiler_params=pltpu.CompilerParams(collective_id=0, has_side_effects=True, vmem_limit_bytes=56 << 20),
+        compiler_params=pltpu.CompilerParams(collective_id=0, has_side_effects=True, vmem_limit_bytes=24 << 20),
         name="hessian",
     )(
-        station_gains.reshape(channels, values, owned),
-        tangent.reshape(channels, values, owned),
-        station_order.reshape(stations // 128, 128),
-        flag_mask,
-        coherency,
+        *(pltpu.with_memory_space_constraint(value, pltpu.HBM) for value in (
+            station_gains.reshape(channels, values, owned),
+            tangent.reshape(channels, values, owned),
+            station_order.reshape(stations // 128, 128),
+            flag_mask,
+            coherency,
+        ))
     )
     return result.reshape(channels, comps, directions, owned)
 

time: 67.2 us -> 62.9 us (0.936)
  Pallas kernels: 65.5 us -> 62 us
  local copies, waits for them, and re-layouts: 1.57 us -> 0.66 us
    pallas_call x1, Pallas kernels: 65.5 us -> 62 us  [on_device(): pl.pallas_call(functools.partial(kernel, groups), out_shape=jax.ShapeDtyp...]
    unnamed x1, local copies, waits for them, and re-layouts: 1.57 us -> 0.66 us
where the time goes in v2:
time: 62.9 us; the launch traced here: 62.6 us
  Pallas kernels  62 us (99%)
  local copies, waits for them, and re-layouts  0.66 us (1%)
    pallas_call x1, Pallas kernels, on_device(): pl.pallas_call(functools.partial(kernel, groups), out_shape=jax.ShapeDtyp...  62 us

profile of v2, /device:TPU:1, one launch (start us, length us, event | category | flops | bytes accessed | tf_op | source)
XLA Modules:
  0.0 62.6 jit_solution(4523117177736357721)
XLA Ops:
  0.0 62.0 %hessian.1 = f32[2,128,16]{2,1,0:T(8,128)S(1)} custom-call(f32[2,128,16]{2,1,0:T(8,128)} %bitcast.5, f32[2,128,16]{2,1,0:T(8,128)} %bitcast.6, s32[4,128]{1,0:T(4,128)} %bitcast.7, s32[64,128]{1,0:T(8,128)} %flag_in.1, bf16[2,8,16,64,128]{4,3,2,1,0:T(8,128)(2,1)} %coh_in.1), custom_call_target="tpu_custom_call" | custom-call | tf_op jit(solution)/shard_map/hessian/pallas_call | solution.py:520
  62.0 0.7 %copy.7 = f32[2,8,16,16]{3,2,1,0:T(8,128)} copy(f32[2,8,16,16]{3,2,1,0:T(8,128)S(1)} %bitcast.4) | data formatting | bytes 32768

commit v3 on v2

--- a/solution.py
+++ b/solution.py
@@ -92,8 +92,8 @@
 def kernel(groups, gain_in, tan_in, order_in, flag_in, coh_in, out_ref,
            gain_ref, tan_ref, order_ref, flag_ref, coh_ref, all_ref, peer_buf, resid_ref,
            pick_ref, place_ref, mix_ref, gj_ref, left_ref, right_ref, row_ref, col_ref,
-           part_ref, from_sib, total, far_buf, near_buf,
-           in_sem, coh_sem, send_z, recv_z, send_s, recv_s, send_g, recv_g, send_w, recv_w, send_f, recv_f, send_n, recv_n):
+           part_ref, from_sib, up_ref, down_ref, own_ref, near_up, near_down, far_up, added_ref, last_ref,
+           in_sem, coh_sem, send_z, recv_z, send_s, recv_s, send_g, recv_g, send_w, recv_w, send_f, recv_f):
     channels, comps, directions, tile_rows, tile_cols = coh_ref.shape
     stations = pick_ref.shape[1]
     values = comps * directions
@@ -144,24 +144,22 @@
                 ))
         return copies
 
-    def to_sibling(channel, offset):
-        slot = HALF + offset
-        return block_copy(channel, -offset, place.core, sibling, send_s.at[channel, slot], recv_s.at[channel, slot])
+    def core_copy(channel, core):
+        return pltpu.make_async_remote_copy(
+            src_ref=all_ref.at[channel, :, core], dst_ref=all_ref.at[channel, :, core],
+            send_sem=send_s.at[channel], recv_sem=recv_s.at[channel], device_id=sibling, device_id_type=MESH,
+        )
 
     def from_ring(channel, offset):
         slot = HALF + offset
         return block_copy(channel, -offset, place.core, sibling, send_z.at[channel, slot], recv_z.at[channel, slot])
 
-    def from_sibling(channel, offset):
-        slot = HALF + offset
-        return block_copy(channel, -offset, 1 - place.core, sibling, send_s.at[channel, slot], recv_s.at[channel, slot])
-
-    offsets = range(1 - HALF, HALF + 1)
     stages = -(-HALF // REACH)
 
     def begin_gather(channel):
-        for copy in pass_on(channel, 1, 0) + pass_on(channel, -1, 0) + [to_sibling(channel, 0)]:
-            copy.start()
+        for pair in zip(pass_on(channel, 1, 0), pass_on(channel, -1, 0)):
+            for copy in pair:
+                copy.start()
 
     def gather_stage(channel, stage):
         for distance in range(min((stage + 1) * REACH, HALF), stage * REACH, -1):
@@ -171,11 +169,11 @@
                     if distance % REACH == 0:
                         for copy in pass_on(channel, way, distance):
                             copy.start()
-                    to_sibling(channel, way * distance).start()
+        if stage == stages - 1:
+            core_copy(channel, place.core).start()
 
     def end_gather(channel):
-        for offset in offsets:
-            from_sibling(channel, offset).wait_recv()
+        core_copy(channel, 1 - place.core).wait_recv()
 
     def to_peer(step):
         return pltpu.make_async_remote_copy(
@@ -184,7 +182,7 @@
         )
 
     def gather_sends(channel):
-        copies = [to_sibling(channel, offset) for offset in offsets]
+        copies = [core_copy(channel, place.core)]
         for way in (1, -1):
             for done in range(0, limit(way), REACH):
                 copies += pass_on(channel, way, done)
@@ -194,10 +192,6 @@
     def rows_of(step):
         chip = place.at(step)
         return chip // NEAR, pl.ds(pl.multiple_of(lax.rem(chip, NEAR) * owned, owned), owned)
-
-    def sums_for(channel, step):
-        run, rows = rows_of(step)
-        return total.at[channel, run, rows, :]
 
     def swap(channel):
         return pltpu.make_async_remote_copy(
@@ -205,61 +199,61 @@
             send_sem=send_w.at[channel], recv_sem=recv_w.at[channel], device_id=sibling, device_id_type=MESH,
         )
 
-    def hop(channel, source, buffer, slot, sends, recvs, step):
+    def hop(source, target, channel, index, step):
         return pltpu.make_async_remote_copy(
-            src_ref=source, dst_ref=buffer.at[channel, slot], send_sem=sends.at[channel, slot], recv_sem=recvs.at[channel, slot],
+            src_ref=source, dst_ref=target, send_sem=send_f.at[channel, index], recv_sem=recv_f.at[channel, index],
             device_id=place.neighbour(step), device_id_type=MESH,
         )
 
-    reaches = ((1, HALF - FAR), (-1, HALF - 1 - FAR))
-
-    def to_add(channel):
-        return {
-            way * step: hop(channel, sums_for(channel, way * (step + FAR)), far_buf, FAR + way * step, send_f, recv_f, way * step)
-            for way, most in reaches for step in range(most, 0, -1)
-        }
-
-    def direct(channel):
-        return {
-            way * step: hop(channel, sums_for(channel, way * step), near_buf, FAR + way * step, send_n, recv_n, way * step)
-            for step in range(1, FAR) for way in (1, -1)
-        }
-
-    def added(channel):
-        return {
-            way * FAR: hop(channel, far_buf.at[channel, FAR if way > 0 else 2 * FAR + 1], near_buf, FAR + way * FAR, send_n, recv_n, way * FAR)
-            for way in (1, -1)
-        }
+    def first_hops(channel):
+        copies = [hop(up_ref.at[channel, 1, FAR - 1], far_up.at[channel], channel, FAR - 1, FAR)]
+        for n in reversed(range(FAR - 1)):
+            copies.append(hop(up_ref.at[channel, :, n], near_up.at[channel, n], channel, n, n + 1))
+            copies.append(hop(down_ref.at[channel, :, n], near_down.at[channel, n], channel, FAR + n, -1 - n))
+        return copies
+
+    def second_hops(channel):
+        return [
+            hop(added_ref.at[channel, n], last_ref.at[channel, n], channel, 2 * FAR - 1 + n, (1 - 2 * n) * FAR) for n in range(2)
+        ]
 
     def send_sums(channel):
         swap(channel).wait_recv()
-        total[channel] = part_ref[channel, :, place.core] + from_sib[channel]
-        for copy in list(to_add(channel).values()) + list(direct(channel).values()):
+        for step in range(1 - HALF, HALF + 1):
+            run, rows = rows_of(step)
+            value = part_ref[channel, run, place.core, rows, :] + from_sib[channel, run, rows, :]
+            if step == 0:
+                own_ref[channel] = value
+            else:
+                side, distance = (up_ref, step - 1) if step > 0 else (down_ref, -step - 1)
+                side[channel, distance // FAR, distance % FAR] = value
+        for copy in first_hops(channel):
             copy.start()
 
     def send_added(channel):
-        arrivals = to_add(channel)
-        for (way, most), copy in zip(reaches, added(channel).values()):
-            run, rows = rows_of(way * FAR)
-            gathered = total[channel, run, rows, :]
-            for step in range(1, most + 1):
-                arrivals[way * step].wait_recv()
-                gathered = gathered + far_buf[channel, FAR + way * step]
-            far_buf[channel, FAR if way > 0 else 2 * FAR + 1] = gathered
+        for copy in first_hops(channel):
+            copy.wait_recv()
+        up = up_ref[channel, 0, FAR - 1] + far_up[channel]
+        down = down_ref[channel, 0, FAR - 1]
+        for n in range(FAR - 1):
+            up = up + near_up[channel, n, 1]
+            down = down + near_down[channel, n, 1]
+        added_ref[channel, 0] = up
+        added_ref[channel, 1] = down
+        for copy in second_hops(channel):
             copy.start()
 
     def finish(channel):
-        run, rows = rows_of(0)
-        summed = total[channel, run, rows, :] + resid_ref[channel]
-        for copy in list(direct(channel).values()) + list(added(channel).values()):
+        summed = own_ref[channel] + resid_ref[channel]
+        for n in range(FAR - 1):
+            summed = summed + near_up[channel, n, 0] + near_down[channel, n, 0]
+        for n, copy in enumerate(second_hops(channel)):
             copy.wait_recv()
-        for slot in range(2 * FAR + 1):
-            if slot != FAR:
-                summed = summed + near_buf[channel, slot]
+            summed = summed + last_ref[channel, n]
         out_ref[channel] = summed.T
 
     def sum_sends(channel):
-        return [swap(channel)] + list(to_add(channel).values()) + list(direct(channel).values()) + list(added(channel).values())
+        return [swap(channel)] + first_hops(channel) + second_hops(channel)
 
 
     basis = smooth_basis(channels * groups)
@@ -453,10 +447,10 @@
     one_hots()
     gather_stage(0, 0)
     begin_gather(1)
+    for stage in range(1, stages):
+        gather_stage(0, stage)
     for step in range(1, groups):
         to_peer(step).start()
-    for stage in range(1, stages):
-        gather_stage(0, stage)
     end_gather(0)
     for copy in coherency:
         copy.wait()
@@ -470,11 +464,11 @@
 
         def one(index, _):
             for stage in range(stages):
-                @pl.when(jnp.logical_and(channel == 0, index == stage))
+                @pl.when(jnp.logical_and(channel == 0, index == 2 * stage))
                 def _():
                     gather_stage(1, stage)
 
-            @pl.when(jnp.logical_and(channel == 1, index == 0))
+            @pl.when(jnp.logical_and(channel == 1, index == 1))
             def _():
                 send_sums(0)
 
@@ -493,13 +487,12 @@
     send_sums(1)
     consensus()
     finish(0)
+    for copy in gather_sends(0) + gather_sends(1) + [to_peer(step) for step in range(1, groups)] + sum_sends(0):
+        copy.wait_send()
     send_added(1)
     finish(1)
-    for channel in range(channels):
-        for copy in gather_sends(channel) + sum_sends(channel):
-            copy.wait_send()
-    for step in range(1, groups):
-        to_peer(step).wait_send()
+    for copy in sum_sends(1):
+        copy.wait_send()
 
 
 def on_device(groups, coherency, station_gains, tangent, flag_mask, station_order):
@@ -541,13 +534,18 @@
             vmem((comps, directions, 8, tile_cols), f32),
             vmem((channels, runs, 2, near, values), f32),
             vmem((channels, runs, near, values), f32),
-            vmem((channels, runs, near, values), f32),
-            vmem((channels, 2 * FAR + 2, owned, values), f32),
-            vmem((channels, 2 * FAR + 1, owned, values), f32),
+            vmem((channels, 2, FAR, owned, values), f32),
+            vmem((channels, 2, FAR, owned, values), f32),
+            vmem((channels, owned, values), f32),
+            vmem((channels, FAR - 1, 2, owned, values), f32),
+            vmem((channels, FAR - 1, 2, owned, values), f32),
+            vmem((channels, owned, values), f32),
+            vmem((channels, 2, owned, values), f32),
+            vmem((channels, 2, owned, values), f32),
             sems(4), sems(channels),
-            sems(channels, CHIPS + 1), sems(channels, CHIPS + 1), sems(channels, CHIPS + 1), sems(channels, CHIPS + 1),
+            sems(channels, CHIPS + 1), sems(channels, CHIPS + 1), sems(channels), sems(channels),
             sems(groups), sems(groups), sems(channels), sems(channels),
-            sems(channels, 2 * FAR + 1), sems(channels, 2 * FAR + 1), sems(channels, 2 * FAR + 1), sems(channels, 2 * FAR + 1),
+            sems(channels, 2 * FAR + 1), sems(channels, 2 * FAR + 1),
         ],
         compiler_params=pltpu.CompilerParams(collective_id=0, has_side_effects=True, vmem_limit_bytes=24 << 20),
         name="hessian",

time: 62.9 us -> 62.6 us (level)
  no operation moved by 1% of the time
where the time goes in v3:
time: 62.6 us; the launch traced here: 62.5 us
  Pallas kernels  61.8 us (99%)
  local copies, waits for them, and re-layouts  0.66 us (1%)
    pallas_call x1, Pallas kernels, on_device(): pl.pallas_call(functools.partial(kernel, groups), out_shape=jax.ShapeDtyp...  61.8 us

profile of v3, /device:TPU:1, one launch (start us, length us, event | category | flops | bytes accessed | tf_op | source)
XLA Modules:
  0.0 62.5 jit_solution(4486926740167030734)
XLA Ops:
  0.0 61.8 %hessian.1 = f32[2,128,16]{2,1,0:T(8,128)S(1)} custom-call(f32[2,128,16]{2,1,0:T(8,128)} %bitcast.5, f32[2,128,16]{2,1,0:T(8,128)} %bitcast.6, s32[4,128]{1,0:T(4,128)} %bitcast.7, s32[64,128]{1,0:T(8,128)} %flag_in.1, bf16[2,8,16,64,128]{4,3,2,1,0:T(8,128)(2,1)} %coh_in.1), custom_call_target="tpu_custom_call" | custom-call | tf_op jit(solution)/shard_map/hessian/pallas_call | solution.py:513
  61.8 0.7 %copy.7 = f32[2,8,16,16]{3,2,1,0:T(8,128)} copy(f32[2,8,16,16]{3,2,1,0:T(8,128)S(1)} %bitcast.4) | data formatting | bytes 32768

commit v4 on v3

--- a/solution.py
+++ b/solution.py
@@ -91,11 +91,12 @@
 
 def kernel(groups, gain_in, tan_in, order_in, flag_in, coh_in, out_ref,
            gain_ref, tan_ref, order_ref, flag_ref, coh_ref, all_ref, peer_buf, resid_ref,
-           pick_ref, place_ref, mix_ref, gj_ref, left_ref, right_ref, row_ref, col_ref,
+           pick_ref, place_ref, chosen_ref, mix_ref, gj_ref, left_ref, right_ref, row_ref, col_ref,
            part_ref, from_sib, up_ref, down_ref, own_ref, near_up, near_down, far_up, added_ref, last_ref,
            in_sem, coh_sem, send_z, recv_z, send_s, recv_s, send_g, recv_g, send_w, recv_w, send_f, recv_f):
     channels, comps, directions, tile_rows, tile_cols = coh_ref.shape
-    stations = pick_ref.shape[1]
+    stations = 2 * pick_ref.shape[2]
+    near = place_ref.shape[2]
     values = comps * directions
     owned = gain_ref.shape[2]
     strips = tile_rows // ROWS
@@ -295,14 +296,24 @@
             turned = ids.astype(jnp.float32).T.astype(jnp.int32)
             count = (tile_cols, tile_rows)[n]
             for tile in range(stations // 128):
-                spot = lax.broadcasted_iota(jnp.int32, (128, 128), 1) + tile * 128
-                pick_ref[n * tile_cols:n * tile_cols + count, tile * 128:(tile + 1) * 128] = as_mask(turned == spot)[:count]
                 spot = lax.broadcasted_iota(jnp.int32, (128, 128), 0) + tile * 128
-                place_ref[tile * 128:(tile + 1) * 128, n * 128:(n + 1) * 128] = as_mask(ids == spot)
+                place_ref[tile, :, :, n * 128:(n + 1) * 128] = as_mask(ids == spot).reshape(2, near, 128)
+            for core in range(2):
+                for tile in range(stations // 256):
+                    lane_in_core = lax.broadcasted_iota(jnp.int32, (128, 128), 1) + tile * 128
+                    spot = (lane_in_core // near) * (2 * near) + core * near + lane_in_core % near
+                    pick_ref[core, n * tile_cols:n * tile_cols + count, tile * 128:(tile + 1) * 128] = as_mask(turned == spot)[:count]
+
+    def chosen_from(channel, core):
+        held = all_ref[channel, :, core].reshape(stations // 2, 2 * values)
+        return [dot(pick_ref[core], part) for part in split(held)]
+
+    def choose_own(channel):
+        for n, value in enumerate(chosen_from(channel, place.core)):
+            chosen_ref[n] = value
 
     def prologue(channel):
-        parts = split(all_ref[channel].reshape(stations, 2 * values))
-        chosen = [dot(pick_ref[...], part) for part in parts]
+        chosen = [chosen_ref[n] + value for n, value in enumerate(chosen_from(channel, 1 - place.core))]
 
         chosen_cols = chosen[0][:tile_cols] + chosen[1][:tile_cols]
         for array in range(2):
@@ -419,13 +430,16 @@
                     by_comp.append(jnp.concatenate(pieces, axis=1))
         row_sums = jnp.concatenate(by_comp, axis=0)
         col_sums = jnp.sum(col_ref[...], axis=2).reshape(values, tile_cols)
-        placed = jnp.zeros((stations, values), jnp.float32)
-        for part in split(jnp.concatenate([col_sums, row_sums], axis=1)):
-            placed = placed + lax.dot_general(
-                place_ref[:, :tile_cols + tile_rows], part, (((1,), (1,)), ((), ())), preferred_element_type=jnp.float32
-            )
-        part_ref[channel] = placed.reshape(part_ref.shape[1:])
+        parts = split(jnp.concatenate([col_sums, row_sums], axis=1))
+
+        def put(core):
+            spots = place_ref[:, core].reshape(stations // 2, 256)[:, :tile_cols + tile_rows]
+            placed = sum(lax.dot_general(spots, part, (((1,), (1,)), ((), ())), preferred_element_type=jnp.float32) for part in parts)
+            part_ref[channel, :, core] = placed.reshape(stations // (2 * near), near, values)
+
+        put(1 - place.core)
         swap(channel).start()
+        put(place.core)
 
 
     inputs[0].wait()
@@ -451,14 +465,15 @@
         gather_stage(0, stage)
     for step in range(1, groups):
         to_peer(step).start()
-    end_gather(0)
     for copy in coherency:
         copy.wait()
 
     def work(channel, _):
-        @pl.when(channel == 1)
-        def _():
-            end_gather(1)
+        choose_own(channel)
+        for ready in range(channels):
+            @pl.when(channel == ready)
+            def _():
+                end_gather(ready)
 
         prologue(channel)
 
@@ -524,8 +539,9 @@
             vmem((channels, runs, 2, near, 2 * values), f32),
             vmem((groups, channels, owned, values), f32),
             vmem((channels, owned, values), f32),
-            vmem((tile_cols + tile_rows, stations), bf16),
-            vmem((stations, 256), bf16),
+            vmem((2, tile_cols + tile_rows, stations // 2), bf16),
+            vmem((runs, 2, near, 256), bf16),
+            vmem((2, tile_cols + tile_rows, 2 * values), f32),
             vmem((strips, comps, directions, 128), f32),
             vmem((24, directions, tile_cols), f32),
             vmem((comps, directions, ROWS, tile_cols), f32),

time: 62.6 us -> 62.5 us (level)
  no operation moved by 1% of the time
where the time goes in v4:
time: 62.5 us; the launch traced here: 62.4 us
  Pallas kernels  61.7 us (99%)
  local copies, waits for them, and re-layouts  0.66 us (1%)
    pallas_call x1, Pallas kernels, on_device(): pl.pallas_call(functools.partial(kernel, groups), out_shape=jax.ShapeDtyp...  61.7 us

profile of v4, /device:TPU:1, one launch (start us, length us, event | category | flops | bytes accessed | tf_op | source)
XLA Modules:
  0.0 62.4 jit_solution(16498694114735078191)
XLA Ops:
  0.0 61.7 %hessian.1 = f32[2,128,16]{2,1,0:T(8,128)S(1)} custom-call(f32[2,128,16]{2,1,0:T(8,128)} %bitcast.5, f32[2,128,16]{2,1,0:T(8,128)} %bitcast.6, s32[4,128]{1,0:T(4,128)} %bitcast.7, s32[64,128]{1,0:T(8,128)} %flag_in.1, bf16[2,8,16,64,128]{4,3,2,1,0:T(8,128)(2,1)} %coh_in.1), custom_call_target="tpu_custom_call" | custom-call | tf_op jit(solution)/shard_map/hessian/pallas_call | solution.py:528
  61.8 0.7 %copy.7 = f32[2,8,16,16]{3,2,1,0:T(8,128)} copy(f32[2,8,16,16]{3,2,1,0:T(8,128)S(1)} %bitcast.4) | data formatting | bytes 32768

commit v5 on v4

--- a/solution.py
+++ b/solution.py
@@ -479,7 +479,7 @@
 
         def one(index, _):
             for stage in range(stages):
-                @pl.when(jnp.logical_and(channel == 0, index == 2 * stage))
+                @pl.when(jnp.logical_and(channel == 0, index == (strips - 1) * stage // (stages - 1)))
                 def _():
                     gather_stage(1, stage)
 
@@ -487,10 +487,6 @@
             def _():
                 send_sums(0)
 
-            @pl.when(jnp.logical_and(channel == 1, index == 3))
-            def _():
-                send_added(0)
-
             strip(channel, index)
             return 0
 
@@ -500,11 +496,14 @@
 
     lax.fori_loop(0, channels, work, 0)
     send_sums(1)
+    send_added(0)
     consensus()
-    finish(0)
-    for copy in gather_sends(0) + gather_sends(1) + [to_peer(step) for step in range(1, groups)] + sum_sends(0):
+    for copy in gather_sends(0) + gather_sends(1) + [to_peer(step) for step in range(1, groups)]:
         copy.wait_send()
     send_added(1)
+    finish(0)
+    for copy in sum_sends(0):
+        copy.wait_send()
     finish(1)
     for copy in sum_sends(1):
         copy.wait_send()

time: 62.5 us -> 59 us (0.944); the launches traced: 62.4 us -> 58 us
  Pallas kernels: 61.7 us -> 57.4 us
    pallas_call x1, Pallas kernels: 61.7 us -> 57.4 us  [on_device(): pl.pallas_call(functools.partial(kernel, groups), out_shape=jax.ShapeDtyp...]
where the time goes in v5:
time: 59 us; the launch traced here: 58 us
  Pallas kernels  57.4 us (97%)
  local copies, waits for them, and re-layouts  0.66 us (1%)
    pallas_call x1, Pallas kernels, on_device(): pl.pallas_call(functools.partial(kernel, groups), out_shape=jax.ShapeDtyp...  57.4 us

profile of v5, /device:TPU:1, one launch (start us, length us, event | category | flops | bytes accessed | tf_op | source)
XLA Modules:
  0.0 58.0 jit_solution(10137344919791667560)
XLA Ops:
  0.0 57.4 %hessian.1 = f32[2,128,16]{2,1,0:T(8,128)S(1)} custom-call(f32[2,128,16]{2,1,0:T(8,128)} %bitcast.5, f32[2,128,16]{2,1,0:T(8,128)} %bitcast.6, s32[4,128]{1,0:T(4,128)} %bitcast.7, s32[64,128]{1,0:T(8,128)} %flag_in.1, bf16[2,8,16,64,128]{4,3,2,1,0:T(8,128)(2,1)} %coh_in.1), custom_call_target="tpu_custom_call" | custom-call | tf_op jit(solution)/shard_map/hessian/pallas_call | solution.py:527
  57.4 0.7 %copy.7 = f32[2,8,16,16]{3,2,1,0:T(8,128)} copy(f32[2,8,16,16]{3,2,1,0:T(8,128)S(1)} %bitcast.4) | data formatting | bytes 32768

commit v6 on v5

--- a/solution.py
+++ b/solution.py
@@ -85,7 +85,7 @@
 ROWS = 16
 
 
-REACH = 4
+REACH = (3, 4)
 FAR = 4
 
 
@@ -114,7 +114,7 @@
     def peer(step):
         return {"grp": lax.rem(grp + (step + groups), groups)}
 
-    partners = [place.neighbour(way * step) for step in range(1, max(REACH, FAR) + 1) for way in (1, -1)]
+    partners = [place.neighbour(way * step) for step in range(1, max(*REACH, FAR) + 1) for way in (1, -1)]
     partners = partners + [sibling] + [peer(step) for step in range(1, groups)]
     barrier = pltpu.get_barrier_semaphore()
     for device in partners:
@@ -137,7 +137,7 @@
 
     def pass_on(channel, way, done):
         copies = []
-        for step in range(REACH, 0, -1):
+        for step in range(REACH[channel], 0, -1):
             if done + step <= limit(way):
                 slot = HALF + way * (done + step)
                 copies.append(block_copy(
@@ -155,7 +155,7 @@
         slot = HALF + offset
         return block_copy(channel, -offset, place.core, sibling, send_z.at[channel, slot], recv_z.at[channel, slot])
 
-    stages = -(-HALF // REACH)
+    stages = [-(-HALF // reach) for reach in REACH]
 
     def begin_gather(channel):
         for pair in zip(pass_on(channel, 1, 0), pass_on(channel, -1, 0)):
@@ -163,14 +163,14 @@
                 copy.start()
 
     def gather_stage(channel, stage):
-        for distance in range(min((stage + 1) * REACH, HALF), stage * REACH, -1):
+        for distance in range(min((stage + 1) * REACH[channel], HALF), stage * REACH[channel], -1):
             for way in (1, -1):
                 if distance <= limit(way):
                     from_ring(channel, way * distance).wait_recv()
-                    if distance % REACH == 0:
+                    if distance % REACH[channel] == 0:
                         for copy in pass_on(channel, way, distance):
                             copy.start()
-        if stage == stages - 1:
+        if stage == stages[channel] - 1:
             core_copy(channel, place.core).start()
 
     def end_gather(channel):
@@ -185,7 +185,7 @@
     def gather_sends(channel):
         copies = [core_copy(channel, place.core)]
         for way in (1, -1):
-            for done in range(0, limit(way), REACH):
+            for done in range(0, limit(way), REACH[channel]):
                 copies += pass_on(channel, way, done)
         return copies
 
@@ -459,9 +459,9 @@
     inputs[2].wait()
     inputs[3].wait()
     one_hots()
-    gather_stage(0, 0)
-    begin_gather(1)
-    for stage in range(1, stages):
+    for stage in range(stages[0]):
+        if stage == stages[0] - 1:
+            begin_gather(1)
         gather_stage(0, stage)
     for step in range(1, groups):
         to_peer(step).start()
@@ -478,8 +478,8 @@
         prologue(channel)
 
         def one(index, _):
-            for stage in range(stages):
-                @pl.when(jnp.logical_and(channel == 0, index == (strips - 1) * stage // (stages - 1)))
+            for stage in range(stages[1]):
+                @pl.when(jnp.logical_and(channel == 0, index == (strips - 1) * stage // (stages[1] - 1)))
                 def _():
                     gather_stage(1, stage)
 

time: 59 us -> 61.1 us (1.036); the launches traced: 58 us -> 61 us
  Pallas kernels: 57.4 us -> 60.3 us
    pallas_call x1, Pallas kernels: 57.4 us -> 60.3 us  [on_device(): pl.pallas_call(functools.partial(kernel, groups), out_shape=jax.ShapeDtyp...]
where the time goes in v6:
time: 61.1 us; the launch traced here: 61 us
  Pallas kernels  60.3 us (99%)
  local copies, waits for them, and re-layouts  0.66 us (1%)
    pallas_call x1, Pallas kernels, on_device(): pl.pallas_call(functools.partial(kernel, groups), out_shape=jax.ShapeDtyp...  60.3 us

profile of v6, /device:TPU:1, one launch (start us, length us, event | category | flops | bytes accessed | tf_op | source)
XLA Modules:
  0.0 61.0 jit_solution(14273911233390113019)
XLA Ops:
  0.0 60.3 %hessian.1 = f32[2,128,16]{2,1,0:T(8,128)S(1)} custom-call(f32[2,128,16]{2,1,0:T(8,128)} %bitcast.5, f32[2,128,16]{2,1,0:T(8,128)} %bitcast.6, s32[4,128]{1,0:T(4,128)} %bitcast.7, s32[64,128]{1,0:T(8,128)} %flag_in.1, bf16[2,8,16,64,128]{4,3,2,1,0:T(8,128)(2,1)} %coh_in.1), custom_call_target="tpu_custom_call" | custom-call | tf_op jit(solution)/shard_map/hessian/pallas_call | solution.py:527
  60.3 0.7 %copy.7 = f32[2,8,16,16]{3,2,1,0:T(8,128)} copy(f32[2,8,16,16]{3,2,1,0:T(8,128)S(1)} %bitcast.4) | data formatting | bytes 32768
